TPU v7x, 512 devices: a whole 4x8x8 slice. The times are simulated.
512 devices in a mesh: fsdp: 16 (over x_lo, y), dp: 32 (over x_hi, z, core).
Axes of the slice: x: 4 (x_hi: 2, x_lo: 2; x = x_hi * 2 + x_lo), y: 8, z: 8, core: 2. Of those that a mesh axis runs over, the one named last changes fastest.
Arguments:
- attn_out: bfloat16 [32768, 8192], P('dp', 'fsdp'), may hold values from -6 to 6
- key_cotangent: bfloat16 [32768, 1024], P('dp'), may hold values from -6 to 6
- key_weight: bfloat16 [8192, 1024], P('fsdp'), may hold values from -0.0625 to 0.0625
- proj_in: bfloat16 [64, 8192], P(None, 'fsdp'), may hold values from -0.0625 to 0.0625
- proj_out: bfloat16 [64, 8192], P(None, 'fsdp'), may hold values from -0.0625 to 0.0625
- query_sketches: bfloat16 [32, 128, 4096], P('dp', 'fsdp'), may hold values from -6 to 6
- block_owner: int32 [32], replicated, may hold values from 0 to 31, each once
- example_ids: int32 [32, 1024], P('dp'), may hold values from 0 to 15, never falling along the last dimension, each value on 1 to 96 neighbouring positions
Outputs:
- scores: float32 [512, 32, 128], P('dp', None, 'fsdp')
Inputs may be any that keep to these rules, and one draw needn't show every extreme that they name: `block_owner`: names every dp index exactly once. `example_ids`: each row numbers the examples of a dp block in order, each 1 to 96 tokens.
All inputs are finite; a program needn't handle non-finite values.
Results may differ from a plain program's by a relative error of at most 0.0003.
Values may be sent and summed in bfloat16 or wider, within the bound.
A program may use at most 64 MiB of HBM per device.

v0:
```python
import jax
import jax.numpy as jnp
from jax import lax
from jax.sharding import PartitionSpec as P

EX = 16


def damped_inverse(gram):
    size = gram.shape[0]
    eye = jnp.eye(size, dtype=jnp.float32)
    damped = gram + 0.1 * jnp.trace(gram) / size * eye
    factor = jnp.linalg.cholesky(damped)
    return jax.scipy.linalg.cho_solve((factor, True), eye)


def condition(inv_out, mats, inv_in):
    return jnp.einsum("ik,nkl,lj->nij", inv_out, mats, inv_in, precision=lax.Precision.HIGHEST)


def on_device(
    attn_out, key_cotangent, key_weight, proj_in, proj_out, query_sketches, block_owner, example_ids
):
    u_part = jnp.dot(attn_out, proj_in.T, preferred_element_type=jnp.float32)
    grad_shard = jnp.dot(key_cotangent, key_weight.T, preferred_element_type=jnp.float32)
    v_part = jnp.dot(grad_shard, proj_out.astype(jnp.float32).T, precision=lax.Precision.HIGHEST)
    u_rows, v_rows = lax.psum((u_part, v_part), "fsdp")
    rank = u_rows.shape[1]
    entries = rank * rank
    labels = jnp.arange(EX, dtype=jnp.int32)
    onehot = (example_ids[0][None, :] == labels[:, None]).astype(jnp.float32)
    weighted_sketch = onehot[:, :, None] * v_rows[None, :, :]
    sketch = jnp.einsum("eti,tj->eij", weighted_sketch, u_rows, precision=lax.Precision.HIGHEST)
    gin_local = jnp.dot(u_rows.T, u_rows, precision=lax.Precision.HIGHEST)
    gout_local = jnp.dot(v_rows.T, v_rows, precision=lax.Precision.HIGHEST)
    gin_total, gout_total = lax.psum((gin_local, gout_local), "dp")
    tokens_all = lax.axis_size("dp") * u_rows.shape[0]
    inv_in = damped_inverse(gin_total / tokens_all)
    inv_out = damped_inverse(gout_total / tokens_all)
    blocks = lax.axis_size("dp")
    per_slice = query_sketches.shape[1]
    training_half = condition(inv_out, sketch, inv_in).reshape(EX, entries)
    empty = jnp.zeros((EX, blocks, per_slice), jnp.float32)
    piece = lax.all_gather(query_sketches, "dp", axis=0, tiled=True)
    count = piece.shape[0]
    rows = piece.reshape(count * per_slice, entries).astype(jnp.float32)
    score_partials = jnp.dot(training_half, rows.T, precision=lax.Precision.HIGHEST)
    score_partials = score_partials.reshape(EX, count, per_slice)
    holders = jnp.arange(count, dtype=jnp.int32)
    select = (block_owner[None, :] == holders[:, None]).astype(jnp.float32)
    totals = empty + jnp.einsum(
        "ekq,kb->ebq", score_partials, select, precision=lax.Precision.HIGHEST
    )
    return totals / entries


def solution(mesh):
    return jax.shard_map(
        on_device,
        mesh=mesh,
        in_specs=(
            P("dp", "fsdp"),
            P("dp", None),
            P("fsdp", None),
            P(None, "fsdp"),
            P(None, "fsdp"),
            P("dp", "fsdp", None),
            P(),
            P("dp", None),
        ),
        out_specs=P("dp", None, "fsdp"),
        check_vma=False,
    )
```

profile of v0, /device:TPU:1, one launch (start us, length us, event | category | flops | bytes accessed | tf_op | source)
XLA Modules:
  0.0 338.5 jit_solution(8623794394492393023)
XLA Ops:
  7.4 1.6 copy-done
  9.0 2.5 fusion.24
  11.5 1.9 fusion.25
  13.4 1.2 fusion.26
  14.7 0.5 all-gather.2.cloned.1.call-update
  15.2 135.9 %all-reduce.4.cloned.1.call-done = (f32[1024,64]{0,1:T(8,128)}, f32[1024,64]{0,1:T(8,128)}) async-done(((f32[1024,64]{0,1:T(8,128)}, f32[1024,64]{0,1:T(8,128)}), (f32[1024,64]{0,1:T(8,128)}, f32[1024,64]{0,1:T(8,128)})) %all-reduce.4.cloned.1.call-update) | async-done | bytes 524304 | tf_op jit(solution)/shard_map/psum | solution.py:27
  151.1 1.5 fusion.27
  152.6 1.4 fusion.29
  154.0 134.1 %all-reduce = (f32[64,64]{0,1:T(8,128)S(1)}, f32[64,64]{0,1:T(8,128)S(1)}) all-reduce(f32[64,64]{0,1:T(8,128)S(1)} %fusion.27, f32[64,64]{0,1:T(8,128)S(1)} %fusion.29), channel_id=1, replica_groups=mesh['fsdp'=16,'dp'=32] {'dp'}, use_global_device_ids=true, to_apply=%region_2.0 | all-reduce | flops 8192 | bytes 65536 | tf_op jit(solution)/shard_map/psum | solution.py:36
  288.1 0.6 select_reduce_fusion.3
  289.4 0.6 select_reduce_fusion.2
  290.7 5.8 %cholesky.55 = f32[64,64]{1,0:T(8,128)S(1)} custom-call(f32[64,64]{1,0:T(8,128)S(1)} %fusion.17), custom_call_target="Cholesky" | custom-call | tf_op jit(solution)/shard_map/jit(cholesky)/cholesky | solution.py:13
  296.6 0.6 compare_reduce_fusion
  297.3 0.7 fusion.14
  297.9 4.9 %custom-call.9 = f32[1,64,64]{1,2,0:T(8,128)S(1)} custom-call(f32[1,64,64]{2,1,0:T(8,128)S(1)} %fusion.14), custom_call_target="InvertDiagBlocksLowerTriangular" | custom-call | tf_op jit(solution)/shard_map/jit(_cho_solve)/triangular_solve | solution.py:14
  302.9 5.8 %cholesky.44 = f32[64,64]{1,0:T(8,128)S(1)} custom-call(f32[64,64]{1,0:T(8,128)S(1)} %fusion.20), custom_call_target="Cholesky" | custom-call | tf_op jit(solution)/shard_map/jit(cholesky)/cholesky | solution.py:13
  308.8 0.6 compare_reduce_fusion.1
  309.5 0.7 fusion.13
  310.1 4.9 %custom-call.8 = f32[1,64,64]{1,2,0:T(8,128)S(1)} custom-call(f32[1,64,64]{2,1,0:T(8,128)S(1)} %fusion.13), custom_call_target="InvertDiagBlocksLowerTriangular" | custom-call | tf_op jit(solution)/shard_map/jit(_cho_solve)/triangular_solve | solution.py:14
  315.9 6.2 %fusion = f32[16,64,64]{1,2,0:T(8,128)S(1)} fusion(f32[1024,64]{0,1:T(8,128)S(1)} %copy-done.2, f32[16,1024]{1,0:T(8,128)S(1)} %fusion.8, f32[1024,64]{0,1:T(8,128)S(1)} %copy-done.3), kind=kOutput, calls=%fused_computation | convolution fusion | flops 806354944 | bytes 851968 | tf_op jit(solution)/shard_map/eti,tj->eij/dot_general | solution.py:33
  322.0 1.6 fusion.28
  323.7 0.6 fusion.30
  324.4 5.8 %fusion.2 = f32[16,32,8]{1,0,2:T(8,128)S(1)} fusion(f32[16,4096,1]{1,0,2:T(8,128)S(1)} %reshape.44, bf16[32,8,4096]{2,1,0:T(8,128)(2,1)} %all-gather.2.cloned.1.call-done), kind=kOutput, calls=%fused_computation.2 | convolution fusion | flops 201326592 | bytes 2375680 | tf_op jit(solution)/shard_map/dot_general | solution.py:47
  330.4 0.7 copy.28
  (33 shorter events, 1.5 us)
Async XLA Ops:
  7.4 1.6 copy-start
  7.4 4.1 %copy-start.4 = (bf16[64,512]{1,0:T(8,128)(2,1)S(1)}, bf16[64,512]{1,0:T(8,128)(2,1)}, u32[]{:S(2)}) copy-start(bf16[64,512]{1,0:T(8,128)(2,1)} %param.15) | copy-start | bytes 196612
  7.4 143.7 %all-reduce.4.cloned.1.call-start = ((), (), s32[]{:S(2)}) async-start(), calls=%async_computation.1 | async-start | bytes 1048576 | tf_op jit(solution)/shard_map/psum | solution.py:27
  11.5 1.9 copy-start.1
  11.5 1.9 copy-start.5
  11.5 3.7 %copy-start.6 = (s32[1,1024]{1,0:T(1,128)S(1)}, s32[1,1024]{1,0:T(1,128)}, u32[]{:S(2)}) copy-start(s32[1,1024]{1,0:T(1,128)} %param.18) | copy-start | bytes 12292
  14.6 309.8 %all-gather.2.cloned.1.call-start = ((), (), s32[]{:S(2)}) async-start(), calls=%async_computation | async-start | bytes 2162688 | tf_op jit(solution)/shard_map/all_gather | solution.py:44
  151.1 164.7 %copy-start.2 = (f32[1024,64]{0,1:T(8,128)S(1)}, f32[1024,64]{0,1:T(8,128)}, u32[]{:S(2)}) copy-start(f32[1024,64]{0,1:T(8,128)} %get-tuple-element.9) | copy-start | bytes 786436
  151.1 164.7 %copy-start.3 = (f32[1024,64]{0,1:T(8,128)S(1)}, f32[1024,64]{0,1:T(8,128)}, u32[]{:S(2)}) copy-start(f32[1024,64]{0,1:T(8,128)} %get-tuple-element.10) | copy-start | bytes 786436
  323.7 6.6 %copy-start.7 = (s32[32]{0:T(128)S(1)}, s32[32]{0:T(128)}, u32[]{:S(2)}) copy-start(s32[32]{0:T(128)} %param.17) | copy-start | bytes 388
Sparse Core Ops, SparseCore 0:
  14.7 136.3 all-reduce.3
Sparse Core Ops, SparseCore 1:
  19.0 92.1 all-gather.1
where the time goes:
time: 342 us; the launch traced here: 339 us
  waiting for transfers between devices  136 us (40%)
  blocking collectives  134 us (39%)
  other arithmetic  25.4 us (7%)
  matrix products  23.5 us (7%)
  between operations  16.4 us (5%)
    psum x1, waiting for transfers between devices, on_device(): u_rows, v_rows = lax.psum((u_part, v_part), 'fsdp')  136 us
    psum x1, blocking collectives, on_device(): gin_total, gout_total = lax.psum((gin_local, gout_local), 'dp')  134 us
    another operation x6, other arithmetic, damped_inverse(): factor = jnp.linalg.cholesky(damped)  13 us
    another operation x4, other arithmetic, damped_inverse(): return jax.scipy.linalg.cho_solve((factor, True), eye)  11.1 us
  transfers between devices with their start and end apart: 2, of which 1 were waited for; matrix products, arithmetic and copies ran while one was open for 11% of the time, Pallas kernels for 0%

commit v1 on v0

v1 whole, which is shorter than its diff:
```python
import functools
import jax
import jax.numpy as jnp
from jax import lax
from jax.experimental import pallas as pl
from jax.experimental.pallas import tpu as pltpu
from jax.sharding import PartitionSpec as P

EX = 16
R = 64
LANES = 128
MESH = pl.DeviceIdType.MESH
NT = (((1,), (1,)), ((), ()))
F32 = jnp.float32
BF16 = jnp.bfloat16


def exact(a, b, dims=(((1,), (0,)), ((), ()))):
    return lax.dot_general(a, b, dims, precision=lax.Precision.HIGHEST, preferred_element_type=F32)


def bf_dot(a, b, dims=(((1,), (0,)), ((), ()))):
    return lax.dot_general(a, b, dims, preferred_element_type=F32)


def halves(x):
    high = x.astype(BF16)
    return high, (x - high.astype(F32)).astype(BF16)


def inverse_pair(gram, eye, left_half, scale):
    diag = jnp.sum(gram * eye, axis=0, keepdims=True) * scale
    tr_in = jnp.sum(jnp.where(left_half, diag, 0.0), axis=1, keepdims=True)
    tr_out = jnp.sum(jnp.where(left_half, 0.0, diag), axis=1, keepdims=True)
    bound = jnp.where(left_half, tr_in, tr_out) * (1.0 + 0.1 / R)
    low = (0.1 / R) / (1.0 + 0.1 / R)
    mat = gram * (scale / bound) + low * eye
    start = 2.0 / (1.0 + low)
    rho = (1.0 - low) / (1.0 + low)
    gain = 2.0 / (2.0 - rho * rho)
    rho = rho * rho / (2.0 - rho * rho)
    prod = start * mat
    turn = 2.0 * eye - prod
    inv = (gain * start) * turn
    prod = gain * exact(prod, turn)
    while rho > 0.05:
        gain = 2.0 / (2.0 - rho * rho)
        rho = rho * rho / (2.0 - rho * rho)
        turn = 2.0 * eye - prod
        both = exact(jnp.concatenate([prod, inv], axis=0), turn) * gain
        prod, inv = both[:LANES], both[LANES:]
    for _ in range(2):
        inv = exact(inv, 2.0 * eye - exact(mat, inv))
    return inv / bound


def kernel(
    nf, nd, tokens_all,
    attn_hbm, cot_hbm, kw_hbm, pin_ref, pout_ref, query_ref, owner_ref, ids_ref,
    out_ref,
    attn, cot, kw, part, rs_buf, chunks, gram_part, ga_buf, gb_own, gb_buf, gfull, qall, select, flat, stage,
    load_sem, rs_send, rs_recv, ag_send, ag_recv, ga_send, ga_recv, gb_send, gb_recv, gc_send, gc_recv,
    q_send, q_recv, sib_send, sib_recv,
):
    f = lax.axis_index("fsdp")
    j = lax.axis_index("dp")
    ntb = nf // 2
    nch = nd // 2
    rows = R // ntb
    core, chip = lax.rem(j, 2), j // 2
    side, block = lax.rem(f, 2), f // 2

    load_attn = pltpu.make_async_copy(attn_hbm, attn, load_sem.at[0])
    load_kw = pltpu.make_async_copy(kw_hbm, kw, load_sem.at[1])
    load_cot = pltpu.make_async_copy(cot_hbm, cot, load_sem.at[2])
    load_attn.start()
    load_kw.start()
    load_cot.start()

    barrier = pltpu.get_barrier_semaphore()

    @pl.loop(1, nf)
    def _(r):
        pl.semaphore_signal(barrier, inc=1, device_id={"fsdp": lax.rem(f + r, nf)}, device_id_type=MESH)

    @pl.loop(1, nd)
    def _(r):
        pl.semaphore_signal(barrier, inc=1, device_id={"dp": lax.rem(j + r, nd)}, device_id_type=MESH)

    half = query_ref.shape[2] // 2
    per = query_ref.shape[1]
    own_q = query_ref[0]
    qall[core, chip] = jnp.concatenate([own_q[:, :half], own_q[:, half:]], axis=0)

    owner = jnp.concatenate([owner_ref[...]] * per, axis=1)
    cols = lax.broadcasted_iota(jnp.int32, select.shape, 1)
    rws = lax.broadcasted_iota(jnp.int32, select.shape, 0)
    holder = lax.rem(rws // (2 * per), nch) * 2 + rws // (2 * per * nch)
    hit = jnp.logical_and(holder == owner, lax.rem(rws, per) == cols // nd)
    select[...] = hit.astype(F32).astype(BF16)

    def scatter(which):
        @pl.loop(0, ntb)
        def _(t):
            dst = 2 * t + which
            slot = lax.rem(dst - f + nf, nf)

            @pl.when(slot > 0)
            def _():
                pltpu.make_async_remote_copy(
                    src_ref=part.at[dst], dst_ref=rs_buf.at[slot - 1], send_sem=rs_send, recv_sem=rs_recv,
                    device_id={"fsdp": dst}, device_id_type=MESH,
                ).start()

    load_attn.wait()
    u_part = bf_dot(pin_ref[...], attn[...], NT)
    for t in range(ntb):
        part[2 * t] = u_part[:, LANES * t:LANES * (t + 1)]
    pl.semaphore_wait(barrier, nf - 1 + nd - 1)
    scatter(0)

    load_kw.wait()
    w_part = bf_dot(pout_ref[...], kw[...])
    w_two = jnp.concatenate(halves(w_part), axis=0)
    load_cot.wait()
    v_two = bf_dot(w_two, cot[...], NT)
    v_part = v_two[:R] + v_two[R:]
    for t in range(ntb):
        part[2 * t + 1] = v_part[:, LANES * t:LANES * (t + 1)]
    scatter(1)

    @pl.loop(1, nch)
    def _(r):
        pltpu.make_async_remote_copy(
            src_ref=qall.at[core, chip], dst_ref=qall.at[core, chip], send_sem=q_send, recv_sem=q_recv,
            device_id={"dp": lax.rem(j + 2 * r, nd)}, device_id_type=MESH,
        ).start()

    row_id = lax.broadcasted_iota(jnp.int32, (LANES, LANES), 0)
    col_id = lax.broadcasted_iota(jnp.int32, (LANES, LANES), 1)
    eye = (row_id == col_id).astype(F32)
    left_half = lax.broadcasted_iota(jnp.int32, (1, LANES), 1) < R

    pltpu.make_async_copy(rs_buf, rs_buf, rs_recv).wait()
    mine = part[f]
    for r in range(nf - 1):
        mine = mine + rs_buf[r]
    chunks[f] = mine

    @pl.loop(1, nf)
    def _(r):
        pltpu.make_async_remote_copy(
            src_ref=chunks.at[f], dst_ref=chunks.at[f], send_sem=ag_send, recv_sem=ag_recv,
            device_id={"fsdp": lax.rem(f + r, nf)}, device_id_type=MESH,
        ).start()

    zero = jnp.zeros_like(mine)
    wide = jnp.concatenate([jnp.where(side == 0, mine, zero), jnp.where(side == 0, zero, mine)], axis=0)
    gram = exact(mine, wide, NT)
    for t in range(ntb):
        gram_part[t] = gram[rows * t:rows * (t + 1)]

    @pl.loop(1, ntb)
    def _(r):
        to = lax.rem(block + r, ntb)
        pltpu.make_async_remote_copy(
            src_ref=gram_part.at[to], dst_ref=ga_buf.at[r - 1], send_sem=ga_send, recv_sem=ga_recv,
            device_id={"fsdp": 2 * to + side}, device_id_type=MESH,
        ).start()

    pltpu.make_async_copy(ga_buf, ga_buf, ga_recv).wait()
    gsum = gram_part[block]
    for r in range(ntb - 1):
        gsum = gsum + ga_buf[r]
    gb_own[...] = gsum

    @pl.loop(1, nd)
    def _(r):
        pltpu.make_async_remote_copy(
            src_ref=gb_own, dst_ref=gb_buf.at[r - 1], send_sem=gb_send, recv_sem=gb_recv,
            device_id={"dp": lax.rem(j + r, nd)}, device_id_type=MESH,
        ).start()

    pltpu.make_async_copy(gb_buf, gb_buf, gb_recv).wait()
    for r in range(nd - 1):
        gsum = gsum + gb_buf[r]
    place = side * ntb + block
    gfull[place] = gsum

    @pl.loop(1, nf)
    def _(r):
        pltpu.make_async_remote_copy(
            src_ref=gfull.at[place], dst_ref=gfull.at[place], send_sem=gc_send, recv_sem=gc_recv,
            device_id={"fsdp": lax.rem(f + r, nf)}, device_id_type=MESH,
        ).start()

    others = qall.at[0, pl.ds(0, nch - 1)]
    pltpu.make_async_copy(others, others, q_recv).wait()
    sibling = pltpu.make_async_remote_copy(
        src_ref=qall.at[core], dst_ref=qall.at[core], send_sem=sib_send, recv_sem=sib_recv,
        device_id={"dp": j + 1 - 2 * core}, device_id_type=MESH,
    )
    sibling.start()

    all_chunks = chunks.at[pl.ds(0, nf - 1)]
    pltpu.make_async_copy(all_chunks, all_chunks, ag_recv).wait()
    u_high, u_low = halves(jnp.concatenate([chunks[2 * t] for t in range(ntb)], axis=1))
    v_high, v_low = halves(jnp.concatenate([chunks[2 * t + 1] for t in range(ntb)], axis=1))
    v_both = jnp.concatenate([v_high, v_low], axis=0)
    ids = ids_ref[...]
    none = jnp.zeros_like(u_high)
    pair = EX // 2
    for p in range(pair):
        marks = [jnp.broadcast_to(ids == e, u_high.shape) for e in (p, p + pair)]
        masked_high = jnp.concatenate([jnp.where(m, u_high, none) for m in marks], axis=0)
        masked_low = jnp.concatenate([jnp.where(m, u_low, none) for m in marks], axis=0)
        top = bf_dot(v_both, masked_high, NT)
        stage[pl.ds(R * p, R), :] = top[:R] + top[R:] + bf_dot(v_high, masked_low, NT)

    all_grams = gfull.at[pl.ds(0, nf - 1)]
    pltpu.make_async_copy(all_grams, all_grams, gc_recv).wait()
    inv = inverse_pair(jnp.concatenate([gfull[t] for t in range(nf)], axis=0), eye, left_half, 1.0 / tokens_all)
    corner = jnp.where(jnp.logical_and(row_id < R, col_id < R), inv, 0.0)
    twice = corner + pltpu.roll(pltpu.roll(corner, R, 0), R, 1)
    right = exact(stage[...], twice)
    right = jnp.concatenate([right[R * p:R * (p + 1)] for p in range(pair)], axis=1)
    both = exact(inv[R:], jnp.concatenate([right, right], axis=0))
    for p in range(pair):
        stage[pl.ds(R * p, R), :] = both[:, LANES * p:LANES * (p + 1)]
    for i in range(R // 2):
        a = stage[pl.ds(2 * i, pair, stride=R), :]
        b = stage[pl.ds(2 * i + 1, pair, stride=R), :]
        low = jnp.where(left_half, a, pltpu.roll(b, R, 1))
        high = jnp.where(left_half, pltpu.roll(a, R, 1), b)
        big, small = halves(jnp.concatenate([low, high], axis=0))
        top, left = (2 * i * R) // half * 2 * EX, (2 * i * R) % half
        flat[pl.ds(top, EX), pl.ds(left, LANES)] = big
        flat[pl.ds(top + EX, EX), pl.ds(left, LANES)] = small

    sibling.wait_recv()
    raw = bf_dot(flat[...], qall[...].reshape(nd * 2 * per, half), NT)
    first = raw[:EX] + raw[EX:2 * EX]
    second = raw[2 * EX:3 * EX] + raw[3 * EX:]
    column = lax.broadcasted_iota(jnp.int32, first.shape, 1)
    sums = jnp.where(lax.rem(column // per, 2) == 0, first, second)
    big = sums.astype(BF16)
    rest = sums - big.astype(F32)
    mid = rest.astype(BF16)
    tail = (rest - mid.astype(F32)).astype(BF16)
    picked = bf_dot(jnp.concatenate([big, mid, tail], axis=0), select[...])
    out_ref[...] = (picked[:EX] + picked[EX:2 * EX] + picked[2 * EX:]) * (1.0 / (R * R))

    sibling.wait_send()
    pltpu.make_async_copy(rs_buf, rs_buf, rs_send).wait()
    pltpu.make_async_copy(all_chunks, all_chunks, ag_send).wait()
    pltpu.make_async_copy(ga_buf, ga_buf, ga_send).wait()
    pltpu.make_async_copy(gb_buf, gb_buf, gb_send).wait()
    pltpu.make_async_copy(all_grams, all_grams, gc_send).wait()
    pltpu.make_async_copy(others, others, q_send).wait()


def on_device(
    nf, nd, attn_out, key_cotangent, key_weight, proj_in, proj_out, query_sketches, block_owner, example_ids
):
    tokens = attn_out.shape[0]
    per = query_sketches.shape[1]
    half = query_sketches.shape[2] // 2
    ntb = nf // 2
    rows = R // ntb
    hbm = pl.BlockSpec(memory_space=pl.ANY)
    vmem = pl.BlockSpec(memory_space=pltpu.VMEM)
    scores = pl.pallas_call(
        functools.partial(kernel, nf, nd, nd * tokens),
        out_shape=jax.ShapeDtypeStruct((EX, per * nd), F32),
        in_specs=[hbm, hbm, hbm, vmem, vmem, vmem, vmem, vmem],
        out_specs=vmem,
        scratch_shapes=[
            pltpu.VMEM(attn_out.shape, BF16),
            pltpu.VMEM(key_cotangent.shape, BF16),
            pltpu.VMEM(key_weight.shape, BF16),
            pltpu.VMEM((nf, R, LANES), F32),
            pltpu.VMEM((nf - 1, R, LANES), F32),
            pltpu.VMEM((nf, R, LANES), F32),
            pltpu.VMEM((ntb, rows, LANES), F32),
            pltpu.VMEM((ntb - 1, rows, LANES), F32),
            pltpu.VMEM((rows, LANES), F32),
            pltpu.VMEM((nd - 1, rows, LANES), F32),
            pltpu.VMEM((nf, rows, LANES), F32),
            pltpu.VMEM((2, nd // 2, 2 * per, half), BF16),
            pltpu.VMEM((nd * 2 * per, per * nd), BF16),
            pltpu.VMEM((4 * EX, half), BF16),
            pltpu.VMEM((EX // 2 * R, LANES), F32),
            pltpu.SemaphoreType.DMA((3,)),
        ] + [pltpu.SemaphoreType.DMA] * 14,
        compiler_params=pltpu.CompilerParams(
            collective_id=0, has_side_effects=True, vmem_limit_bytes=40 * 1024 * 1024
        ),
        name="influence",
    )(
        attn_out, key_cotangent, key_weight, proj_in, proj_out, query_sketches,
        block_owner.reshape(1, nd), example_ids,
    )
    return scores.reshape(EX, per, nd).transpose(0, 2, 1)


def solution(mesh):
    return jax.shard_map(
        functools.partial(on_device, mesh.shape["fsdp"], mesh.shape["dp"]),
        mesh=mesh,
        in_specs=(
            P("dp", "fsdp"),
            P("dp", None),
            P("fsdp", None),
            P(None, "fsdp"),
            P(None, "fsdp"),
            P("dp", "fsdp", None),
            P(),
            P("dp", None),
        ),
        out_specs=P("dp", None, "fsdp"),
        check_vma=False,
    )
```

time: 342 us -> 71.7 us (0.21)
  waiting for transfers between devices: 136 us -> 0 us
  blocking collectives: 134 us -> 0 us
  Pallas kernels: 0 us -> 62.7 us
  other arithmetic: 25.4 us -> 0 us
  matrix products: 23.5 us -> 0 us
  between operations: 16.4 us -> 0.02 us
  local copies, waits for them, and re-layouts: 2.62 us -> 8.61 us
    psum x1 -> x0, waiting for transfers between devices: 136 us -> none  [on_device(): u_rows, v_rows = lax.psum((u_part, v_part), 'fsdp')]
    psum x1 -> x0, blocking collectives: 134 us -> none  [on_device(): gin_total, gout_total = lax.psum((gin_local, gout_local), 'dp')]
    pallas_call x0 -> x1, Pallas kernels: none -> 62.7 us  [on_device(): pl.pallas_call(functools.partial(kernel, nf, nd, nd * tokens), out_shape=...]
    another operation x10 -> x0, other arithmetic: 24.1 us -> none  [the longest x6 13 us: damped_inverse(): factor = jnp.linalg.cholesky(damped)]
    dot_general x10 -> x0, matrix products: 22.7 us -> none  [the longest x1 6.18 us: on_device(): jnp.einsum('eti,tj->eij', weighted_sketch, u_rows, precision=lax.Precisio...]
    unnamed x16, local copies, waits for them, and re-layouts: 1.62 us -> 7.9 us
  transfers between devices with their start and end apart: 2 -> 0, of which waited for: 1 -> 0; matrix products, arithmetic and copies ran while one was open for 11% -> 0% of each run, Pallas kernels for 0% -> 0%
where the time goes in v1:
time: 71.7 us; the launch traced here: 71.3 us
  Pallas kernels  62.7 us (87%)
  local copies, waits for them, and re-layouts  8.61 us (12%)
    pallas_call x1, Pallas kernels, on_device(): pl.pallas_call(functools.partial(kernel, nf, nd, nd * tokens), out_shape=...  62.7 us
    unnamed x16, local copies, waits for them, and re-layouts  7.9 us

profile of v1, /device:TPU:1, one launch (start us, length us, event | category | flops | bytes accessed | tf_op | source)
XLA Modules:
  0.0 71.3 jit_solution(13905067770985972824)
XLA Ops:
  0.0 0.0 copy-start
  0.0 1.6 %copy-done = bf16[1024,1024]{1,0:T(8,128)(2,1)S(1)} copy-done((bf16[1024,1024]{1,0:T(8,128)(2,1)S(1)}, bf16[1024,1024]{1,0:T(8,128)(2,1)}, u32[]{:S(2)}) %copy-start) | copy-done | bytes 2097176
  1.6 0.0 copy-start.1
  1.6 1.2 %copy-done.1 = bf16[1024,512]{1,0:T(8,128)(2,1)S(1)} copy-done((bf16[1024,512]{1,0:T(8,128)(2,1)S(1)}, bf16[1024,512]{1,0:T(8,128)(2,1)}, u32[]{:S(2)}) %copy-start.1) | copy-done | bytes 1048600
  2.8 0.0 copy-start.2
  2.8 1.2 %copy-done.2 = bf16[512,1024]{1,0:T(8,128)(2,1)S(1)} copy-done((bf16[512,1024]{1,0:T(8,128)(2,1)S(1)}, bf16[512,1024]{1,0:T(8,128)(2,1)}, u32[]{:S(2)}) %copy-start.2) | copy-done | bytes 1048600
  4.0 0.0 copy-start.3
  4.0 0.8 %copy-done.3 = bf16[64,512]{1,0:T(8,128)(2,1)S(1)} copy-done((bf16[64,512]{1,0:T(8,128)(2,1)S(1)}, bf16[64,512]{1,0:T(8,128)(2,1)}, u32[]{:S(2)}) %copy-start.3) | copy-done | bytes 65560
  4.9 0.0 copy-start.4
  4.9 0.8 %copy-done.4 = bf16[64,512]{1,0:T(8,128)(2,1)S(1)} copy-done((bf16[64,512]{1,0:T(8,128)(2,1)S(1)}, bf16[64,512]{1,0:T(8,128)(2,1)}, u32[]{:S(2)}) %copy-start.4) | copy-done | bytes 65560
  5.7 0.0 copy-start.5
  5.7 0.8 %copy-done.5 = bf16[1,8,4096]{2,1,0:T(8,128)(2,1)S(1)} copy-done((bf16[1,8,4096]{2,1,0:T(8,128)(2,1)S(1)}, bf16[1,8,4096]{2,1,0:T(8,128)(2,1)}, u32[]{:S(2)}) %copy-start.5) | copy-done | bytes 65560
  6.6 0.0 copy-start.6
  6.6 0.7 copy-done.6
  7.2 0.0 copy-start.7
  7.3 0.7 copy-done.7
  7.9 62.7 %influence.1 = f32[16,256]{1,0:T(8,128)S(1)} custom-call(bf16[1024,512]{1,0:T(8,128)(2,1)S(1)} %copy-done.1, bf16[1024,1024]{1,0:T(8,128)(2,1)S(1)} %copy-done, bf16[512,1024]{1,0:T(8,128)(2,1)S(1)} %copy-done.2, bf16[64,512]{1,0:T(8,128)(2,1)S(1)} %copy-done.3, bf16[64,512]{1,0:T(8,128)(2,1)S(1)} %copy-done.4, bf16[1,8,4096]{2,1,0:T(8,128)(2,1)S(1)} %copy-done.5, ...), custom_call_target="tpu_custom_call" | custom-call | tf_op jit(solution)/shard_map/influence/pallas_call | solution.py:272
  70.6 0.7 reshape.7
Async XLA Ops:
  0.0 1.6 %copy-start = (bf16[1024,1024]{1,0:T(8,128)(2,1)S(1)}, bf16[1024,1024]{1,0:T(8,128)(2,1)}, u32[]{:S(2)}) copy-start(bf16[1024,1024]{1,0:T(8,128)(2,1)} %cot_hbm.1) | copy-start | bytes 6291460
  1.6 1.2 %copy-start.1 = (bf16[1024,512]{1,0:T(8,128)(2,1)S(1)}, bf16[1024,512]{1,0:T(8,128)(2,1)}, u32[]{:S(2)}) copy-start(bf16[1024,512]{1,0:T(8,128)(2,1)} %attn_hbm.1) | copy-start | bytes 3145732
  2.8 1.2 %copy-start.2 = (bf16[512,1024]{1,0:T(8,128)(2,1)S(1)}, bf16[512,1024]{1,0:T(8,128)(2,1)}, u32[]{:S(2)}) copy-start(bf16[512,1024]{1,0:T(8,128)(2,1)} %kw_hbm.1) | copy-start | bytes 3145732
  4.0 0.8 %copy-start.3 = (bf16[64,512]{1,0:T(8,128)(2,1)S(1)}, bf16[64,512]{1,0:T(8,128)(2,1)}, u32[]{:S(2)}) copy-start(bf16[64,512]{1,0:T(8,128)(2,1)} %pin_ref.1) | copy-start | bytes 196612
  4.9 0.8 %copy-start.4 = (bf16[64,512]{1,0:T(8,128)(2,1)S(1)}, bf16[64,512]{1,0:T(8,128)(2,1)}, u32[]{:S(2)}) copy-start(bf16[64,512]{1,0:T(8,128)(2,1)} %pout_ref.1) | copy-start | bytes 196612
  5.7 0.8 %copy-start.5 = (bf16[1,8,4096]{2,1,0:T(8,128)(2,1)S(1)}, bf16[1,8,4096]{2,1,0:T(8,128)(2,1)}, u32[]{:S(2)}) copy-start(bf16[1,8,4096]{2,1,0:T(8,128)(2,1)} %query_ref.1) | copy-start | bytes 196612
  6.6 0.7 copy-start.6
  7.2 0.7 copy-start.7

commit v2 on v1

--- a/solution.py
+++ b/solution.py
@@ -56,9 +56,9 @@
 
 def kernel(
     nf, nd, tokens_all,
-    attn_hbm, cot_hbm, kw_hbm, pin_ref, pout_ref, query_ref, owner_ref, ids_ref,
+    attn_hbm, cot_hbm, kw_hbm, pin_hbm, pout_hbm, query_hbm, owner_hbm, ids_hbm,
     out_ref,
-    attn, cot, kw, part, rs_buf, chunks, gram_part, ga_buf, gb_own, gb_buf, gfull, qall, select, flat, stage,
+    attn, cot, kw, pin_ref, pout_ref, query_ref, owner_ref, ids_ref, part, rs_buf, chunks, gram_part, ga_buf, gb_own, gb_buf, gfull, qall, select, flat, stage,
     load_sem, rs_send, rs_recv, ag_send, ag_recv, ga_send, ga_recv, gb_send, gb_recv, gc_send, gc_recv,
     q_send, q_recv, sib_send, sib_recv,
 ):
@@ -71,11 +71,15 @@
     side, block = lax.rem(f, 2), f // 2
 
     load_attn = pltpu.make_async_copy(attn_hbm, attn, load_sem.at[0])
-    load_kw = pltpu.make_async_copy(kw_hbm, kw, load_sem.at[1])
-    load_cot = pltpu.make_async_copy(cot_hbm, cot, load_sem.at[2])
-    load_attn.start()
-    load_kw.start()
-    load_cot.start()
+    load_pin = pltpu.make_async_copy(pin_hbm, pin_ref, load_sem.at[1])
+    load_kw = pltpu.make_async_copy(kw_hbm, kw, load_sem.at[2])
+    load_pout = pltpu.make_async_copy(pout_hbm, pout_ref, load_sem.at[3])
+    load_cot = pltpu.make_async_copy(cot_hbm, cot, load_sem.at[4])
+    load_query = pltpu.make_async_copy(query_hbm, query_ref, load_sem.at[5])
+    load_owner = pltpu.make_async_copy(owner_hbm, owner_ref, load_sem.at[6])
+    load_ids = pltpu.make_async_copy(ids_hbm, ids_ref, load_sem.at[7])
+    for load in (load_attn, load_pin, load_kw, load_pout, load_cot, load_query, load_owner, load_ids):
+        load.start()
 
     barrier = pltpu.get_barrier_semaphore()
 
@@ -89,6 +93,8 @@
 
     half = query_ref.shape[2] // 2
     per = query_ref.shape[1]
+    load_query.wait()
+    load_owner.wait()
     own_q = query_ref[0]
     qall[core, chip] = jnp.concatenate([own_q[:, :half], own_q[:, half:]], axis=0)
 
@@ -113,6 +119,7 @@
                 ).start()
 
     load_attn.wait()
+    load_pin.wait()
     u_part = bf_dot(pin_ref[...], attn[...], NT)
     for t in range(ntb):
         part[2 * t] = u_part[:, LANES * t:LANES * (t + 1)]
@@ -120,6 +127,7 @@
     scatter(0)
 
     load_kw.wait()
+    load_pout.wait()
     w_part = bf_dot(pout_ref[...], kw[...])
     w_two = jnp.concatenate(halves(w_part), axis=0)
     load_cot.wait()
@@ -207,6 +215,7 @@
     u_high, u_low = halves(jnp.concatenate([chunks[2 * t] for t in range(ntb)], axis=1))
     v_high, v_low = halves(jnp.concatenate([chunks[2 * t + 1] for t in range(ntb)], axis=1))
     v_both = jnp.concatenate([v_high, v_low], axis=0)
+    load_ids.wait()
     ids = ids_ref[...]
     none = jnp.zeros_like(u_high)
     pair = EX // 2
@@ -272,12 +281,17 @@
     scores = pl.pallas_call(
         functools.partial(kernel, nf, nd, nd * tokens),
         out_shape=jax.ShapeDtypeStruct((EX, per * nd), F32),
-        in_specs=[hbm, hbm, hbm, vmem, vmem, vmem, vmem, vmem],
+        in_specs=[hbm] * 8,
         out_specs=vmem,
         scratch_shapes=[
             pltpu.VMEM(attn_out.shape, BF16),
             pltpu.VMEM(key_cotangent.shape, BF16),
             pltpu.VMEM(key_weight.shape, BF16),
+            pltpu.VMEM(proj_in.shape, BF16),
+            pltpu.VMEM(proj_out.shape, BF16),
+            pltpu.VMEM(query_sketches.shape, BF16),
+            pltpu.VMEM((1, nd), jnp.int32),
+            pltpu.VMEM(example_ids.shape, jnp.int32),
             pltpu.VMEM((nf, R, LANES), F32),
             pltpu.VMEM((nf - 1, R, LANES), F32),
             pltpu.VMEM((nf, R, LANES), F32),
@@ -290,10 +304,10 @@
             pltpu.VMEM((nd * 2 * per, per * nd), BF16),
             pltpu.VMEM((4 * EX, half), BF16),
             pltpu.VMEM((EX // 2 * R, LANES), F32),
-            pltpu.SemaphoreType.DMA((3,)),
+            pltpu.SemaphoreType.DMA((8,)),
         ] + [pltpu.SemaphoreType.DMA] * 14,
         compiler_params=pltpu.CompilerParams(
-            collective_id=0, has_side_effects=True, vmem_limit_bytes=40 * 1024 * 1024
+            collective_id=0, has_side_effects=True, vmem_limit_bytes=62 * 1024 * 1024
         ),
         name="influence",
     )(

time: 71.7 us -> 64.2 us (0.90)
  local copies, waits for them, and re-layouts: 8.61 us -> 1.43 us
    unnamed x16 -> x0, local copies, waits for them, and re-layouts: 7.9 us -> none
    reshape x1, local copies, waits for them, and re-layouts: 0.71 us -> 1.43 us  [on_device(): return scores.reshape(EX, per, nd).transpose(0, 2, 1)]
where the time goes in v2:
time: 64.2 us; the launch traced here: 64 us
  Pallas kernels  62.5 us (97%)
  local copies, waits for them, and re-layouts  1.43 us (2%)
    pallas_call x1, Pallas kernels, on_device(): pl.pallas_call(functools.partial(kernel, nf, nd, nd * tokens), out_shape=...  62.5 us
    reshape x1, local copies, waits for them, and re-layouts, on_device(): return scores.reshape(EX, per, nd).transpose(0, 2, 1)  1.43 us

profile of v2, /device:TPU:1, one launch (start us, length us, event | category | flops | bytes accessed | tf_op | source)
XLA Modules:
  0.0 64.0 jit_solution(3083402008190139940)
XLA Ops:
  0.0 62.5 %influence.1 = f32[16,256]{1,0:T(8,128)} custom-call(bf16[1024,512]{1,0:T(8,128)(2,1)} %attn_hbm.1, bf16[1024,1024]{1,0:T(8,128)(2,1)} %cot_hbm.1, bf16[512,1024]{1,0:T(8,128)(2,1)} %kw_hbm.1, bf16[64,512]{1,0:T(8,128)(2,1)} %pin_hbm.1, bf16[64,512]{1,0:T(8,128)(2,1)} %pout_hbm.1, bf16[1,8,4096]{2,1,0:T(8,128)(2,1)} %query_hbm.1, s32[1,32]{1,0:T(1,128)} %bitcast.2, ...), custom_call_target="tpu_custom_call" | custom-call | tf_op jit(solution)/shard_map/influence/pallas_call | solution.py:281
  62.6 1.4 %reshape.7 = f32[16,8,32]{2,1,0:T(8,128)} reshape(f32[16,256]{1,0:T(8,128)} %influence.1) | data formatting | bytes 32768 | tf_op jit(solution)/shard_map/reshape | solution.py:317

commit v3 on v2

--- a/solution.py
+++ b/solution.py
@@ -54,14 +54,18 @@
     return inv / bound
 
 
+def by_distance(steps, far):
+    return sorted(steps, key=lambda r: -far(r))
+
+
 def kernel(
     nf, nd, tokens_all,
     attn_hbm, cot_hbm, kw_hbm, pin_hbm, pout_hbm, query_hbm, owner_hbm, ids_hbm,
     out_ref,
-    attn, cot, kw, pin_ref, pout_ref, query_ref, owner_ref, ids_ref, part, rs_buf, chunks, gram_part, ga_buf, gb_own, gb_buf, gfull, qall, select, flat, stage,
-    load_sem, rs_send, rs_recv, ag_send, ag_recv, ga_send, ga_recv, gb_send, gb_recv, gc_send, gc_recv,
-    q_send, q_recv, sib_send, sib_recv,
+    attn, cot, kw, pin_ref, pout_ref, query_ref, owner_ref, ids_ref, part, rs_buf, chunks, gram_part, ga_buf, gs_buf, gb_own, gb_buf, gfull, qall, select, flat, stage,
+    load_sem, *sems,
 ):
+    rs_sems, ag_sems, ga_sems, gs_sems, gb_sems, gc_sems, x_sems, q_sems, p_sems, sib_sems = zip(sems[::2], sems[1::2])
     f = lax.axis_index("fsdp")
     j = lax.axis_index("dp")
     ntb = nf // 2
@@ -69,6 +73,8 @@
     rows = R // ntb
     core, chip = lax.rem(j, 2), j // 2
     side, block = lax.rem(f, 2), f // 2
+    half = query_ref.shape[2] // 2
+    per = query_ref.shape[1]
 
     load_attn = pltpu.make_async_copy(attn_hbm, attn, load_sem.at[0])
     load_pin = pltpu.make_async_copy(pin_hbm, pin_ref, load_sem.at[1])
@@ -81,49 +87,46 @@
     for load in (load_attn, load_pin, load_kw, load_pout, load_cot, load_query, load_owner, load_ids):
         load.start()
 
+    ny, nz = nf // 2, nd // 4
+    f_far = lambda r: min(r % ny, ny - r % ny) + (r >= ny)
+    z_far = lambda r: min(r % nz, nz - r % nz) + 2 * (r >= nz)
+    f_steps = by_distance(range(1, nf), f_far)
+    d_steps = by_distance(range(1, nch), z_far)
+    sibling = {"dp": j + 1 - 2 * core}
+    over_f = lambda r: {"fsdp": lax.rem(f + r, nf)}
+    over_d = lambda r: {"dp": lax.rem(j + 2 * r, nd)}
+
     barrier = pltpu.get_barrier_semaphore()
-
-    @pl.loop(1, nf)
-    def _(r):
-        pl.semaphore_signal(barrier, inc=1, device_id={"fsdp": lax.rem(f + r, nf)}, device_id_type=MESH)
-
-    @pl.loop(1, nd)
-    def _(r):
-        pl.semaphore_signal(barrier, inc=1, device_id={"dp": lax.rem(j + r, nd)}, device_id_type=MESH)
-
-    half = query_ref.shape[2] // 2
-    per = query_ref.shape[1]
-    load_query.wait()
-    load_owner.wait()
-    own_q = query_ref[0]
-    qall[core, chip] = jnp.concatenate([own_q[:, :half], own_q[:, half:]], axis=0)
-
-    owner = jnp.concatenate([owner_ref[...]] * per, axis=1)
-    cols = lax.broadcasted_iota(jnp.int32, select.shape, 1)
-    rws = lax.broadcasted_iota(jnp.int32, select.shape, 0)
-    holder = lax.rem(rws // (2 * per), nch) * 2 + rws // (2 * per * nch)
-    hit = jnp.logical_and(holder == owner, lax.rem(rws, per) == cols // nd)
-    select[...] = hit.astype(F32).astype(BF16)
+    for peer in [over_d(r) for r in d_steps] + [over_f(r) for r in f_steps] + [sibling]:
+        pl.semaphore_signal(barrier, inc=1, device_id=peer, device_id_type=MESH)
+
+    def send(src, dst, sems, peer):
+        copy = pltpu.make_async_remote_copy(
+            src_ref=src, dst_ref=dst, send_sem=sems[0], recv_sem=sems[1], device_id=peer, device_id_type=MESH
+        )
+        copy.start()
+        return copy
+
+    even = by_distance(range(0, nf, 2), f_far)
+    odd = by_distance(range(1, nf, 2), f_far)
+    even = [r for r in even if r] + [0]
 
     def scatter(which):
-        @pl.loop(0, ntb)
-        def _(t):
-            dst = 2 * t + which
-            slot = lax.rem(dst - f + nf, nf)
-
-            @pl.when(slot > 0)
+        other = side != which
+        for r_even, r_odd in zip(even, odd):
+            r = jnp.where(other, r_odd, r_even)
+            dst = lax.rem(f + r, nf)
+
+            @pl.when(r > 0)
             def _():
-                pltpu.make_async_remote_copy(
-                    src_ref=part.at[dst], dst_ref=rs_buf.at[slot - 1], send_sem=rs_send, recv_sem=rs_recv,
-                    device_id={"fsdp": dst}, device_id_type=MESH,
-                ).start()
+                send(part.at[dst], rs_buf.at[r - 1], rs_sems, {"fsdp": dst})
 
     load_attn.wait()
     load_pin.wait()
     u_part = bf_dot(pin_ref[...], attn[...], NT)
     for t in range(ntb):
         part[2 * t] = u_part[:, LANES * t:LANES * (t + 1)]
-    pl.semaphore_wait(barrier, nf - 1 + nd - 1)
+    pl.semaphore_wait(barrier, nf - 1 + nch)
     scatter(0)
 
     load_kw.wait()
@@ -137,30 +140,40 @@
         part[2 * t + 1] = v_part[:, LANES * t:LANES * (t + 1)]
     scatter(1)
 
-    @pl.loop(1, nch)
-    def _(r):
-        pltpu.make_async_remote_copy(
-            src_ref=qall.at[core, chip], dst_ref=qall.at[core, chip], send_sem=q_send, recv_sem=q_recv,
-            device_id={"dp": lax.rem(j + 2 * r, nd)}, device_id_type=MESH,
-        ).start()
+    load_query.wait()
+    own_q = query_ref[0]
+    z, x = lax.rem(chip, nz), chip // nz
+    partner = 1 - x
+    qall[core, z, x] = jnp.concatenate([own_q[:, :half], own_q[:, half:]], axis=0)
+    across = send(qall.at[core, z, x], qall.at[core, z, x], x_sems, {"dp": lax.rem(j + nch, nd)})
+    z_steps = by_distance(range(1, nz), z_far)
+    along_z = lambda r: {"dp": (x * nz + lax.rem(z + r, nz)) * 2 + core}
+    for r in z_steps:
+        send(qall.at[core, z, x], qall.at[core, z, x], q_sems, along_z(r))
+
+    load_owner.wait()
+    owner = jnp.concatenate([owner_ref[...]] * per, axis=1)
+    cols = lax.broadcasted_iota(jnp.int32, select.shape, 1)
+    rws = lax.broadcasted_iota(jnp.int32, select.shape, 0)
+    block_of = rws // (2 * per)
+    holder = (lax.rem(block_of, 2) * nz + lax.rem(block_of // 2, nz)) * 2 + block_of // nch
+    hit = jnp.logical_and(holder == owner, lax.rem(rws, per) == cols // nd)
+    select[...] = hit.astype(F32).astype(BF16)
+
+    across.wait_recv()
+    for r in z_steps:
+        send(qall.at[core, z, partner], qall.at[core, z, partner], p_sems, along_z(r))
 
     row_id = lax.broadcasted_iota(jnp.int32, (LANES, LANES), 0)
     col_id = lax.broadcasted_iota(jnp.int32, (LANES, LANES), 1)
     eye = (row_id == col_id).astype(F32)
     left_half = lax.broadcasted_iota(jnp.int32, (1, LANES), 1) < R
 
-    pltpu.make_async_copy(rs_buf, rs_buf, rs_recv).wait()
+    pltpu.make_async_copy(rs_buf, rs_buf, rs_sems[1]).wait()
     mine = part[f]
     for r in range(nf - 1):
         mine = mine + rs_buf[r]
     chunks[f] = mine
-
-    @pl.loop(1, nf)
-    def _(r):
-        pltpu.make_async_remote_copy(
-            src_ref=chunks.at[f], dst_ref=chunks.at[f], send_sem=ag_send, recv_sem=ag_recv,
-            device_id={"fsdp": lax.rem(f + r, nf)}, device_id_type=MESH,
-        ).start()
 
     zero = jnp.zeros_like(mine)
     wide = jnp.concatenate([jnp.where(side == 0, mine, zero), jnp.where(side == 0, zero, mine)], axis=0)
@@ -168,50 +181,40 @@
     for t in range(ntb):
         gram_part[t] = gram[rows * t:rows * (t + 1)]
 
-    @pl.loop(1, ntb)
-    def _(r):
+    for r in by_distance(range(1, ntb), lambda r: f_far(2 * r)):
         to = lax.rem(block + r, ntb)
-        pltpu.make_async_remote_copy(
-            src_ref=gram_part.at[to], dst_ref=ga_buf.at[r - 1], send_sem=ga_send, recv_sem=ga_recv,
-            device_id={"fsdp": 2 * to + side}, device_id_type=MESH,
-        ).start()
-
-    pltpu.make_async_copy(ga_buf, ga_buf, ga_recv).wait()
+        send(gram_part.at[to], ga_buf.at[r - 1], ga_sems, {"fsdp": 2 * to + side})
+    for r in f_steps:
+        send(chunks.at[f], chunks.at[f], ag_sems, over_f(r))
+
+    pltpu.make_async_copy(ga_buf, ga_buf, ga_sems[1]).wait()
     gsum = gram_part[block]
     for r in range(ntb - 1):
         gsum = gsum + ga_buf[r]
-    gb_own[...] = gsum
-
-    @pl.loop(1, nd)
-    def _(r):
-        pltpu.make_async_remote_copy(
-            src_ref=gb_own, dst_ref=gb_buf.at[r - 1], send_sem=gb_send, recv_sem=gb_recv,
-            device_id={"dp": lax.rem(j + r, nd)}, device_id_type=MESH,
-        ).start()
-
-    pltpu.make_async_copy(gb_buf, gb_buf, gb_recv).wait()
-    for r in range(nd - 1):
+    gb_own[0] = gsum
+    twin = send(gb_own.at[0], gs_buf, gs_sems, sibling)
+    twin.wait_recv()
+    gsum = gsum + gs_buf[...]
+    gb_own[1] = gsum
+    for r in d_steps:
+        send(gb_own.at[1], gb_buf.at[r - 1], gb_sems, over_d(r))
+
+    pltpu.make_async_copy(gb_buf, gb_buf, gb_sems[1]).wait()
+    for r in range(nch - 1):
         gsum = gsum + gb_buf[r]
     place = side * ntb + block
     gfull[place] = gsum
 
-    @pl.loop(1, nf)
-    def _(r):
-        pltpu.make_async_remote_copy(
-            src_ref=gfull.at[place], dst_ref=gfull.at[place], send_sem=gc_send, recv_sem=gc_recv,
-            device_id={"fsdp": lax.rem(f + r, nf)}, device_id_type=MESH,
-        ).start()
-
-    others = qall.at[0, pl.ds(0, nch - 1)]
-    pltpu.make_async_copy(others, others, q_recv).wait()
-    sibling = pltpu.make_async_remote_copy(
-        src_ref=qall.at[core], dst_ref=qall.at[core], send_sem=sib_send, recv_sem=sib_recv,
-        device_id={"dp": j + 1 - 2 * core}, device_id_type=MESH,
-    )
-    sibling.start()
+    for r in f_steps:
+        send(gfull.at[place], gfull.at[place], gc_sems, over_f(r))
+
+    blocks = qall.at[0, pl.ds(0, nz - 1), 0]
+    pltpu.make_async_copy(blocks, blocks, q_sems[1]).wait()
+    pltpu.make_async_copy(blocks, blocks, p_sems[1]).wait()
+    twin_q = send(qall.at[core], qall.at[core], sib_sems, sibling)
 
     all_chunks = chunks.at[pl.ds(0, nf - 1)]
-    pltpu.make_async_copy(all_chunks, all_chunks, ag_recv).wait()
+    pltpu.make_async_copy(all_chunks, all_chunks, ag_sems[1]).wait()
     u_high, u_low = halves(jnp.concatenate([chunks[2 * t] for t in range(ntb)], axis=1))
     v_high, v_low = halves(jnp.concatenate([chunks[2 * t + 1] for t in range(ntb)], axis=1))
     v_both = jnp.concatenate([v_high, v_low], axis=0)
@@ -227,7 +230,7 @@
         stage[pl.ds(R * p, R), :] = top[:R] + top[R:] + bf_dot(v_high, masked_low, NT)
 
     all_grams = gfull.at[pl.ds(0, nf - 1)]
-    pltpu.make_async_copy(all_grams, all_grams, gc_recv).wait()
+    pltpu.make_async_copy(all_grams, all_grams, gc_sems[1]).wait()
     inv = inverse_pair(jnp.concatenate([gfull[t] for t in range(nf)], axis=0), eye, left_half, 1.0 / tokens_all)
     corner = jnp.where(jnp.logical_and(row_id < R, col_id < R), inv, 0.0)
     twice = corner + pltpu.roll(pltpu.roll(corner, R, 0), R, 1)
@@ -246,7 +249,7 @@
         flat[pl.ds(top, EX), pl.ds(left, LANES)] = big
         flat[pl.ds(top + EX, EX), pl.ds(left, LANES)] = small
 
-    sibling.wait_recv()
+    twin_q.wait_recv()
     raw = bf_dot(flat[...], qall[...].reshape(nd * 2 * per, half), NT)
     first = raw[:EX] + raw[EX:2 * EX]
     second = raw[2 * EX:3 * EX] + raw[3 * EX:]
@@ -257,15 +260,18 @@
     mid = rest.astype(BF16)
     tail = (rest - mid.astype(F32)).astype(BF16)
     picked = bf_dot(jnp.concatenate([big, mid, tail], axis=0), select[...])
-    out_ref[...] = (picked[:EX] + picked[EX:2 * EX] + picked[2 * EX:]) * (1.0 / (R * R))
-
-    sibling.wait_send()
-    pltpu.make_async_copy(rs_buf, rs_buf, rs_send).wait()
-    pltpu.make_async_copy(all_chunks, all_chunks, ag_send).wait()
-    pltpu.make_async_copy(ga_buf, ga_buf, ga_send).wait()
-    pltpu.make_async_copy(gb_buf, gb_buf, gb_send).wait()
-    pltpu.make_async_copy(all_grams, all_grams, gc_send).wait()
-    pltpu.make_async_copy(others, others, q_send).wait()
+    picked = (picked[:EX] + picked[EX:2 * EX] + picked[2 * EX:]) * (1.0 / (R * R))
+    for i in range(per):
+        out_ref[:, i, :] = picked[:, nd * i:nd * (i + 1)]
+
+    across.wait_send()
+    twin.wait_send()
+    twin_q.wait_send()
+    for buf, sems in (
+        (rs_buf, rs_sems), (all_chunks, ag_sems), (ga_buf, ga_sems), (gb_buf, gb_sems), (all_grams, gc_sems),
+        (blocks, q_sems), (blocks, p_sems),
+    ):
+        pltpu.make_async_copy(buf, buf, sems[0]).wait()
 
 
 def on_device(
@@ -280,7 +286,7 @@
     vmem = pl.BlockSpec(memory_space=pltpu.VMEM)
     scores = pl.pallas_call(
         functools.partial(kernel, nf, nd, nd * tokens),
-        out_shape=jax.ShapeDtypeStruct((EX, per * nd), F32),
+        out_shape=jax.ShapeDtypeStruct((EX, per, nd), F32),
         in_specs=[hbm] * 8,
         out_specs=vmem,
         scratch_shapes=[
@@ -298,14 +304,15 @@
             pltpu.VMEM((ntb, rows, LANES), F32),
             pltpu.VMEM((ntb - 1, rows, LANES), F32),
             pltpu.VMEM((rows, LANES), F32),
-            pltpu.VMEM((nd - 1, rows, LANES), F32),
+            pltpu.VMEM((2, rows, LANES), F32),
+            pltpu.VMEM((nd // 2 - 1, rows, LANES), F32),
             pltpu.VMEM((nf, rows, LANES), F32),
-            pltpu.VMEM((2, nd // 2, 2 * per, half), BF16),
+            pltpu.VMEM((2, nd // 4, 2, 2 * per, half), BF16),
             pltpu.VMEM((nd * 2 * per, per * nd), BF16),
             pltpu.VMEM((4 * EX, half), BF16),
             pltpu.VMEM((EX // 2 * R, LANES), F32),
             pltpu.SemaphoreType.DMA((8,)),
-        ] + [pltpu.SemaphoreType.DMA] * 14,
+        ] + [pltpu.SemaphoreType.DMA] * 20,
         compiler_params=pltpu.CompilerParams(
             collective_id=0, has_side_effects=True, vmem_limit_bytes=62 * 1024 * 1024
         ),
@@ -314,7 +321,7 @@
         attn_out, key_cotangent, key_weight, proj_in, proj_out, query_sketches,
         block_owner.reshape(1, nd), example_ids,
     )
-    return scores.reshape(EX, per, nd).transpose(0, 2, 1)
+    return scores.transpose(0, 2, 1)
 
 
 def solution(mesh):

time: 64.2 us -> 56.9 us (0.89)
  the two profiles are of different devices: /device:TPU:1 before, /device:TPU:4 now
where the time goes in v3:
time: 56.9 us; the launch traced here: 56.7 us
  Pallas kernels  55.2 us (97%)
  local copies, waits for them, and re-layouts  1.47 us (3%)
    pallas_call x1, Pallas kernels, on_device(): pl.pallas_call(functools.partial(kernel, nf, nd, nd * tokens), out_shape=...  55.2 us
    unnamed x1, local copies, waits for them, and re-layouts  1.47 us

profile of v3, /device:TPU:4, one launch (start us, length us, event | category | flops | bytes accessed | tf_op | source)
XLA Modules:
  0.0 56.7 jit_solution(11440809547809385467)
XLA Ops:
  0.0 55.2 %influence.1 = f32[16,8,32]{2,1,0:T(8,128)} custom-call(bf16[1024,512]{1,0:T(8,128)(2,1)} %attn_hbm.1, bf16[1024,1024]{1,0:T(8,128)(2,1)} %cot_hbm.1, bf16[512,1024]{1,0:T(8,128)(2,1)} %kw_hbm.1, bf16[64,512]{1,0:T(8,128)(2,1)} %pin_hbm.1, bf16[64,512]{1,0:T(8,128)(2,1)} %pout_hbm.1, bf16[1,8,4096]{2,1,0:T(8,128)(2,1)} %query_hbm.1, s32[1,32]{1,0:T(1,128)} %bitcast.3, ...), custom_call_target="tpu_custom_call" | custom-call | tf_op jit(solution)/shard_map/influence/pallas_call | solution.py:287
  55.2 1.5 %copy.10 = f32[16,32,8]{1,2,0:T(8,128)} copy(f32[16,32,8]{1,2,0:T(8,128)} %bitcast.2) | data formatting | bytes 32768

commit v4 on v3

--- a/solution.py
+++ b/solution.py
@@ -26,6 +26,18 @@
 def halves(x):
     high = x.astype(BF16)
     return high, (x - high.astype(F32)).astype(BF16)
+
+
+def three(a, b):
+    a_high, a_low = halves(a)
+    b_high, b_low = halves(b)
+    return bf_dot(jnp.concatenate([a_high, a_low, a_high], axis=1), jnp.concatenate([b_high, b_high, b_low], axis=0))
+
+
+def split_ring(n):
+    near = [d for d in (n - 2, 2, n - 1, 1) if 0 < d < n]
+    near = sorted(set(near), key=near.index)
+    return near, [d for d in (n // 2, n // 2 - 1, n // 2 + 1) if 0 < d < n and d not in near]
 
 
 def inverse_pair(gram, eye, left_half, scale):
@@ -42,15 +54,15 @@
     prod = start * mat
     turn = 2.0 * eye - prod
     inv = (gain * start) * turn
-    prod = gain * exact(prod, turn)
+    prod = gain * three(prod, turn)
     while rho > 0.05:
         gain = 2.0 / (2.0 - rho * rho)
         rho = rho * rho / (2.0 - rho * rho)
         turn = 2.0 * eye - prod
-        both = exact(jnp.concatenate([prod, inv], axis=0), turn) * gain
+        both = three(jnp.concatenate([prod, inv], axis=0), turn) * gain
         prod, inv = both[:LANES], both[LANES:]
     for _ in range(2):
-        inv = exact(inv, 2.0 * eye - exact(mat, inv))
+        inv = inv + three(inv, eye - exact(mat, inv))
     return inv / bound
 
 
@@ -62,10 +74,13 @@
     nf, nd, tokens_all,
     attn_hbm, cot_hbm, kw_hbm, pin_hbm, pout_hbm, query_hbm, owner_hbm, ids_hbm,
     out_ref,
-    attn, cot, kw, pin_ref, pout_ref, query_ref, owner_ref, ids_ref, part, rs_buf, chunks, gram_part, ga_buf, gs_buf, gb_own, gb_buf, gfull, qall, select, flat, stage,
+    attn, cot, kw, pin_ref, pout_ref, query_ref, owner_ref, ids_ref, part, cross, joint, rs_buf, chunks, gram_part, ga_buf, gs_buf, gb_own, gb_buf, gfull, qall, select, flat, stage,
     load_sem, *sems,
 ):
-    rs_sems, ag_sems, ga_sems, gs_sems, gb_sems, gc_sems, x_sems, q_sems, p_sems, sib_sems = zip(sems[::2], sems[1::2])
+    (
+        rs_sems, cross_sems, ag_sems, far_sems, hand_sems, ga_sems, gs_sems, gb_sems, gc_sems,
+        x_sems, q_sems, p_sems, q2_sems, p2_sems, sib_sems,
+    ) = zip(sems[::2], sems[1::2])
     f = lax.axis_index("fsdp")
     j = lax.axis_index("dp")
     ntb = nf // 2
@@ -107,27 +122,11 @@
         copy.start()
         return copy
 
-    even = by_distance(range(0, nf, 2), f_far)
-    odd = by_distance(range(1, nf, 2), f_far)
-    even = [r for r in even if r] + [0]
-
-    def scatter(which):
-        other = side != which
-        for r_even, r_odd in zip(even, odd):
-            r = jnp.where(other, r_odd, r_even)
-            dst = lax.rem(f + r, nf)
-
-            @pl.when(r > 0)
-            def _():
-                send(part.at[dst], rs_buf.at[r - 1], rs_sems, {"fsdp": dst})
-
     load_attn.wait()
     load_pin.wait()
     u_part = bf_dot(pin_ref[...], attn[...], NT)
     for t in range(ntb):
         part[2 * t] = u_part[:, LANES * t:LANES * (t + 1)]
-    pl.semaphore_wait(barrier, nf - 1 + nch)
-    scatter(0)
 
     load_kw.wait()
     load_pout.wait()
@@ -138,7 +137,20 @@
     v_part = v_two[:R] + v_two[R:]
     for t in range(ntb):
         part[2 * t + 1] = v_part[:, LANES * t:LANES * (t + 1)]
-    scatter(1)
+    pl.semaphore_wait(barrier, nf - 1 + nch)
+
+    col, y = f // ny, lax.rem(f, ny)
+    place_of = lambda c, d: c * ny + lax.rem(y + d, ny)
+    near, far = split_ring(ny)
+    other = 1 - col
+    pair_f = {"fsdp": place_of(other, 0)}
+    for k, d in enumerate(far):
+        send(part.at[place_of(other, d)], cross.at[k], cross_sems, pair_f)
+    for k, d in enumerate(near):
+        for i, c in enumerate((other, col)):
+            to = place_of(c, d)
+            send(part.at[to], rs_buf.at[1 + 2 * k + i], rs_sems, {"fsdp": to})
+    send(part.at[place_of(other, 0)], rs_buf.at[0], rs_sems, pair_f)
 
     load_query.wait()
     own_q = query_ref[0]
@@ -146,10 +158,33 @@
     partner = 1 - x
     qall[core, z, x] = jnp.concatenate([own_q[:, :half], own_q[:, half:]], axis=0)
     across = send(qall.at[core, z, x], qall.at[core, z, x], x_sems, {"dp": lax.rem(j + nch, nd)})
-    z_steps = by_distance(range(1, nz), z_far)
-    along_z = lambda r: {"dp": (x * nz + lax.rem(z + r, nz)) * 2 + core}
-    for r in z_steps:
-        send(qall.at[core, z, x], qall.at[core, z, x], q_sems, along_z(r))
+    z_near, z_rest = split_ring(nz)
+
+    def hand(origin, c, d, pair_sems):
+        block = qall.at[core, lax.rem(z + origin, nz), c]
+        send(block, block, pair_sems, {"dp": (x * nz + lax.rem(z + d, nz)) * 2 + core})
+
+    def await_blocks(count, sem):
+        if count:
+            some = qall.at[0, pl.ds(0, count), 0]
+            pltpu.make_async_copy(some, some, sem).wait()
+
+    def onward(c, near_sems, rest_sems):
+        await_blocks(len(z_near), near_sems[1])
+        if z_rest:
+            hand(nz - 2, c, 2, rest_sems)
+            hand(nz - 2, c, 1, rest_sems)
+            hand(2, c, nz - 1, rest_sems)
+
+    for d in z_near:
+        hand(0, x, d, q_sems)
+
+    if far:
+        pltpu.make_async_copy(cross, cross, cross_sems[1]).wait()
+    for k, d in enumerate(far):
+        to = place_of(col, d)
+        joint[k] = part[to] + cross[k]
+        send(joint.at[k], rs_buf.at[1 + 2 * len(near) + k], rs_sems, {"fsdp": to})
 
     load_owner.wait()
     owner = jnp.concatenate([owner_ref[...]] * per, axis=1)
@@ -161,8 +196,10 @@
     select[...] = hit.astype(F32).astype(BF16)
 
     across.wait_recv()
-    for r in z_steps:
-        send(qall.at[core, z, partner], qall.at[core, z, partner], p_sems, along_z(r))
+    for d in z_near:
+        hand(0, partner, d, p_sems)
+    onward(x, q_sems, q2_sems)
+    onward(partner, p_sems, p2_sems)
 
     row_id = lax.broadcasted_iota(jnp.int32, (LANES, LANES), 0)
     col_id = lax.broadcasted_iota(jnp.int32, (LANES, LANES), 1)
@@ -171,7 +208,7 @@
 
     pltpu.make_async_copy(rs_buf, rs_buf, rs_sems[1]).wait()
     mine = part[f]
-    for r in range(nf - 1):
+    for r in range(rs_buf.shape[0]):
         mine = mine + rs_buf[r]
     chunks[f] = mine
 
@@ -184,8 +221,12 @@
     for r in by_distance(range(1, ntb), lambda r: f_far(2 * r)):
         to = lax.rem(block + r, ntb)
         send(gram_part.at[to], ga_buf.at[r - 1], ga_sems, {"fsdp": 2 * to + side})
-    for r in f_steps:
-        send(chunks.at[f], chunks.at[f], ag_sems, over_f(r))
+    for d in far:
+        send(chunks.at[f], chunks.at[f], far_sems, {"fsdp": place_of(col, d)})
+    for d in near:
+        for c in (other, col):
+            send(chunks.at[f], chunks.at[f], ag_sems, {"fsdp": place_of(c, d)})
+    send(chunks.at[f], chunks.at[f], ag_sems, pair_f)
 
     pltpu.make_async_copy(ga_buf, ga_buf, ga_sems[1]).wait()
     gsum = gram_part[block]
@@ -198,6 +239,12 @@
     gb_own[1] = gsum
     for r in d_steps:
         send(gb_own.at[1], gb_buf.at[r - 1], gb_sems, over_d(r))
+    far_chunks = chunks.at[pl.ds(0, len(far))]
+    if far:
+        pltpu.make_async_copy(far_chunks, far_chunks, far_sems[1]).wait()
+    for d in far:
+        held = chunks.at[place_of(col, d)]
+        send(held, held, hand_sems, pair_f)
 
     pltpu.make_async_copy(gb_buf, gb_buf, gb_sems[1]).wait()
     for r in range(nch - 1):
@@ -208,13 +255,14 @@
     for r in f_steps:
         send(gfull.at[place], gfull.at[place], gc_sems, over_f(r))
 
-    blocks = qall.at[0, pl.ds(0, nz - 1), 0]
-    pltpu.make_async_copy(blocks, blocks, q_sems[1]).wait()
-    pltpu.make_async_copy(blocks, blocks, p_sems[1]).wait()
+    await_blocks(len(z_rest), q2_sems[1])
+    await_blocks(len(z_rest), p2_sems[1])
     twin_q = send(qall.at[core], qall.at[core], sib_sems, sibling)
 
-    all_chunks = chunks.at[pl.ds(0, nf - 1)]
-    pltpu.make_async_copy(all_chunks, all_chunks, ag_sems[1]).wait()
+    near_chunks = chunks.at[pl.ds(0, 1 + 2 * len(near))]
+    pltpu.make_async_copy(near_chunks, near_chunks, ag_sems[1]).wait()
+    if far:
+        pltpu.make_async_copy(far_chunks, far_chunks, hand_sems[1]).wait()
     u_high, u_low = halves(jnp.concatenate([chunks[2 * t] for t in range(ntb)], axis=1))
     v_high, v_low = halves(jnp.concatenate([chunks[2 * t + 1] for t in range(ntb)], axis=1))
     v_both = jnp.concatenate([v_high, v_low], axis=0)
@@ -234,9 +282,9 @@
     inv = inverse_pair(jnp.concatenate([gfull[t] for t in range(nf)], axis=0), eye, left_half, 1.0 / tokens_all)
     corner = jnp.where(jnp.logical_and(row_id < R, col_id < R), inv, 0.0)
     twice = corner + pltpu.roll(pltpu.roll(corner, R, 0), R, 1)
-    right = exact(stage[...], twice)
+    right = three(stage[...], twice)
     right = jnp.concatenate([right[R * p:R * (p + 1)] for p in range(pair)], axis=1)
-    both = exact(inv[R:], jnp.concatenate([right, right], axis=0))
+    both = three(inv[R:], jnp.concatenate([right, right], axis=0))
     for p in range(pair):
         stage[pl.ds(R * p, R), :] = both[:, LANES * p:LANES * (p + 1)]
     for i in range(R // 2):
@@ -267,11 +315,16 @@
     across.wait_send()
     twin.wait_send()
     twin_q.wait_send()
-    for buf, sems in (
-        (rs_buf, rs_sems), (all_chunks, ag_sems), (ga_buf, ga_sems), (gb_buf, gb_sems), (all_grams, gc_sems),
-        (blocks, q_sems), (blocks, p_sems),
+    for buf, pair_sems in (
+        (rs_buf, rs_sems), (near_chunks, ag_sems), (ga_buf, ga_sems), (gb_buf, gb_sems), (all_grams, gc_sems),
     ):
-        pltpu.make_async_copy(buf, buf, sems[0]).wait()
+        pltpu.make_async_copy(buf, buf, pair_sems[0]).wait()
+    if far:
+        pltpu.make_async_copy(cross, cross, cross_sems[0]).wait()
+        pltpu.make_async_copy(far_chunks, far_chunks, far_sems[0]).wait()
+        pltpu.make_async_copy(far_chunks, far_chunks, hand_sems[0]).wait()
+    for count, pair_sems in ((z_near, q_sems), (z_near, p_sems), (z_rest, q2_sems), (z_rest, p2_sems)):
+        await_blocks(len(count), pair_sems[0])
 
 
 def on_device(
@@ -282,6 +335,7 @@
     half = query_sketches.shape[2] // 2
     ntb = nf // 2
     rows = R // ntb
+    far = len(split_ring(ntb)[1])
     hbm = pl.BlockSpec(memory_space=pl.ANY)
     vmem = pl.BlockSpec(memory_space=pltpu.VMEM)
     scores = pl.pallas_call(
@@ -299,7 +353,9 @@
             pltpu.VMEM((1, nd), jnp.int32),
             pltpu.VMEM(example_ids.shape, jnp.int32),
             pltpu.VMEM((nf, R, LANES), F32),
-            pltpu.VMEM((nf - 1, R, LANES), F32),
+            pltpu.VMEM((max(1, far), R, LANES), F32),
+            pltpu.VMEM((max(1, far), R, LANES), F32),
+            pltpu.VMEM((nf - 1 - far, R, LANES), F32),
             pltpu.VMEM((nf, R, LANES), F32),
             pltpu.VMEM((ntb, rows, LANES), F32),
             pltpu.VMEM((ntb - 1, rows, LANES), F32),
@@ -312,7 +368,7 @@
             pltpu.VMEM((4 * EX, half), BF16),
             pltpu.VMEM((EX // 2 * R, LANES), F32),
             pltpu.SemaphoreType.DMA((8,)),
-        ] + [pltpu.SemaphoreType.DMA] * 20,
+        ] + [pltpu.SemaphoreType.DMA] * 30,
         compiler_params=pltpu.CompilerParams(
             collective_id=0, has_side_effects=True, vmem_limit_bytes=62 * 1024 * 1024
         ),

time: 56.9 us -> 55.5 us (0.975)
  the two profiles are of different devices: /device:TPU:4 before, /device:TPU:1 now
where the time goes in v4:
time: 55.5 us; the launch traced here: 55.3 us
  Pallas kernels  53.8 us (97%)
  local copies, waits for them, and re-layouts  1.47 us (3%)
    pallas_call x1, Pallas kernels, on_device(): pl.pallas_call(functools.partial(kernel, nf, nd, nd * tokens), out_shape=...  53.8 us
    unnamed x1, local copies, waits for them, and re-layouts  1.47 us

profile of v4, /device:TPU:1, one launch (start us, length us, event | category | flops | bytes accessed | tf_op | source)
XLA Modules:
  0.0 55.3 jit_solution(15647513867027683301)
XLA Ops:
  0.0 53.8 %influence.1 = f32[16,8,32]{2,1,0:T(8,128)} custom-call(bf16[1024,512]{1,0:T(8,128)(2,1)} %attn_hbm.1, bf16[1024,1024]{1,0:T(8,128)(2,1)} %cot_hbm.1, bf16[512,1024]{1,0:T(8,128)(2,1)} %kw_hbm.1, bf16[64,512]{1,0:T(8,128)(2,1)} %pin_hbm.1, bf16[64,512]{1,0:T(8,128)(2,1)} %pout_hbm.1, bf16[1,8,4096]{2,1,0:T(8,128)(2,1)} %query_hbm.1, s32[1,32]{1,0:T(1,128)} %bitcast.3, ...), custom_call_target="tpu_custom_call" | custom-call | tf_op jit(solution)/shard_map/influence/pallas_call | solution.py:341
  53.9 1.5 %copy.10 = f32[16,32,8]{1,2,0:T(8,128)} copy(f32[16,32,8]{1,2,0:T(8,128)} %bitcast.2) | data formatting | bytes 32768

commit v5 on v4

--- a/solution.py
+++ b/solution.py
@@ -75,7 +75,7 @@
     attn_hbm, cot_hbm, kw_hbm, pin_hbm, pout_hbm, query_hbm, owner_hbm, ids_hbm,
     out_ref,
     attn, cot, kw, pin_ref, pout_ref, query_ref, owner_ref, ids_ref, part, cross, joint, rs_buf, chunks, gram_part, ga_buf, gs_buf, gb_own, gb_buf, gfull, qall, select, flat, stage,
-    load_sem, *sems,
+    load_sem, relay, *sems,
 ):
     (
         rs_sems, cross_sems, ag_sems, far_sems, hand_sems, ga_sems, gs_sems, gb_sems, gc_sems,
@@ -111,8 +111,20 @@
     over_f = lambda r: {"fsdp": lax.rem(f + r, nf)}
     over_d = lambda r: {"dp": lax.rem(j + 2 * r, nd)}
 
+    col, y = f // ny, lax.rem(f, ny)
+    place_of = lambda c, d: c * ny + lax.rem(y + d, ny)
+    near, far = split_ring(ny)
+    other = 1 - col
+    pair_f = {"fsdp": place_of(other, 0)}
+    z, x = lax.rem(chip, nz), chip // nz
+    partner = 1 - x
+    z_near, z_rest = split_ring(nz)
+    over_z = lambda d: {"dp": (x * nz + lax.rem(z + d, nz)) * 2 + core}
+    pair_d = {"dp": lax.rem(j + nch, nd)}
+    greeted = [pair_f, pair_d, sibling] + [over_z(d) for d in z_near]
+    greeted += [{"fsdp": place_of(c, d)} for d in near for c in (other, col)]
     barrier = pltpu.get_barrier_semaphore()
-    for peer in [over_d(r) for r in d_steps] + [over_f(r) for r in f_steps] + [sibling]:
+    for peer in reversed(greeted):
         pl.semaphore_signal(barrier, inc=1, device_id=peer, device_id_type=MESH)
 
     def send(src, dst, sems, peer):
@@ -137,13 +149,11 @@
     v_part = v_two[:R] + v_two[R:]
     for t in range(ntb):
         part[2 * t + 1] = v_part[:, LANES * t:LANES * (t + 1)]
-    pl.semaphore_wait(barrier, nf - 1 + nch)
-
-    col, y = f // ny, lax.rem(f, ny)
-    place_of = lambda c, d: c * ny + lax.rem(y + d, ny)
-    near, far = split_ring(ny)
-    other = 1 - col
-    pair_f = {"fsdp": place_of(other, 0)}
+    pl.semaphore_wait(barrier, len(greeted))
+    relays = [2, ny - 2] if far else []
+    for d in relays:
+        pl.semaphore_signal(relay, inc=1, device_id={"fsdp": place_of(col, d)}, device_id_type=MESH)
+
     for k, d in enumerate(far):
         send(part.at[place_of(other, d)], cross.at[k], cross_sems, pair_f)
     for k, d in enumerate(near):
@@ -154,15 +164,12 @@
 
     load_query.wait()
     own_q = query_ref[0]
-    z, x = lax.rem(chip, nz), chip // nz
-    partner = 1 - x
     qall[core, z, x] = jnp.concatenate([own_q[:, :half], own_q[:, half:]], axis=0)
-    across = send(qall.at[core, z, x], qall.at[core, z, x], x_sems, {"dp": lax.rem(j + nch, nd)})
-    z_near, z_rest = split_ring(nz)
+    across = send(qall.at[core, z, x], qall.at[core, z, x], x_sems, pair_d)
 
     def hand(origin, c, d, pair_sems):
         block = qall.at[core, lax.rem(z + origin, nz), c]
-        send(block, block, pair_sems, {"dp": (x * nz + lax.rem(z + d, nz)) * 2 + core})
+        send(block, block, pair_sems, over_z(d))
 
     def await_blocks(count, sem):
         if count:
@@ -180,6 +187,7 @@
         hand(0, x, d, q_sems)
 
     if far:
+        pl.semaphore_wait(relay, len(relays))
         pltpu.make_async_copy(cross, cross, cross_sems[1]).wait()
     for k, d in enumerate(far):
         to = place_of(col, d)
@@ -199,7 +207,6 @@
     for d in z_near:
         hand(0, partner, d, p_sems)
     onward(x, q_sems, q2_sems)
-    onward(partner, p_sems, p2_sems)
 
     row_id = lax.broadcasted_iota(jnp.int32, (LANES, LANES), 0)
     col_id = lax.broadcasted_iota(jnp.int32, (LANES, LANES), 1)
@@ -228,6 +235,7 @@
             send(chunks.at[f], chunks.at[f], ag_sems, {"fsdp": place_of(c, d)})
     send(chunks.at[f], chunks.at[f], ag_sems, pair_f)
 
+    onward(partner, p_sems, p2_sems)
     pltpu.make_async_copy(ga_buf, ga_buf, ga_sems[1]).wait()
     gsum = gram_part[block]
     for r in range(ntb - 1):
@@ -368,6 +376,7 @@
             pltpu.VMEM((4 * EX, half), BF16),
             pltpu.VMEM((EX // 2 * R, LANES), F32),
             pltpu.SemaphoreType.DMA((8,)),
+            pltpu.SemaphoreType.REGULAR,
         ] + [pltpu.SemaphoreType.DMA] * 30,
         compiler_params=pltpu.CompilerParams(
             collective_id=0, has_side_effects=True, vmem_limit_bytes=62 * 1024 * 1024

time: 55.5 us -> 52.6 us (0.948)
  Pallas kernels: 53.8 us -> 50.9 us
    pallas_call x1, Pallas kernels: 53.8 us -> 50.9 us  [on_device(): pl.pallas_call(functools.partial(kernel, nf, nd, nd * tokens), out_shape=...]
where the time goes in v5:
time: 52.6 us; the launch traced here: 52.4 us
  Pallas kernels  50.9 us (97%)
  local copies, waits for them, and re-layouts  1.47 us (3%)
    pallas_call x1, Pallas kernels, on_device(): pl.pallas_call(functools.partial(kernel, nf, nd, nd * tokens), out_shape=...  50.9 us
    unnamed x1, local copies, waits for them, and re-layouts  1.47 us

profile of v5, /device:TPU:1, one launch (start us, length us, event | category | flops | bytes accessed | tf_op | source)
XLA Modules:
  0.0 52.4 jit_solution(15520828372781081304)
XLA Ops:
  0.0 50.9 %influence.1 = f32[16,8,32]{2,1,0:T(8,128)} custom-call(bf16[1024,512]{1,0:T(8,128)(2,1)} %attn_hbm.1, bf16[1024,1024]{1,0:T(8,128)(2,1)} %cot_hbm.1, bf16[512,1024]{1,0:T(8,128)(2,1)} %kw_hbm.1, bf16[64,512]{1,0:T(8,128)(2,1)} %pin_hbm.1, bf16[64,512]{1,0:T(8,128)(2,1)} %pout_hbm.1, bf16[1,8,4096]{2,1,0:T(8,128)(2,1)} %query_hbm.1, s32[1,32]{1,0:T(1,128)} %bitcast.3, ...), custom_call_target="tpu_custom_call" | custom-call | tf_op jit(solution)/shard_map/influence/pallas_call | solution.py:349
  50.9 1.5 %copy.10 = f32[16,32,8]{1,2,0:T(8,128)} copy(f32[16,32,8]{1,2,0:T(8,128)} %bitcast.2) | data formatting | bytes 32768

commit v6 on v5

--- a/solution.py
+++ b/solution.py
@@ -87,7 +87,7 @@
     nch = nd // 2
     rows = R // ntb
     core, chip = lax.rem(j, 2), j // 2
-    side, block = lax.rem(f, 2), f // 2
+    side, block = f // ntb, lax.rem(f, ntb)
     half = query_ref.shape[2] // 2
     per = query_ref.shape[1]
 
@@ -138,7 +138,7 @@
     load_pin.wait()
     u_part = bf_dot(pin_ref[...], attn[...], NT)
     for t in range(ntb):
-        part[2 * t] = u_part[:, LANES * t:LANES * (t + 1)]
+        part[t] = u_part[:, LANES * t:LANES * (t + 1)]
 
     load_kw.wait()
     load_pout.wait()
@@ -148,7 +148,7 @@
     v_two = bf_dot(w_two, cot[...], NT)
     v_part = v_two[:R] + v_two[R:]
     for t in range(ntb):
-        part[2 * t + 1] = v_part[:, LANES * t:LANES * (t + 1)]
+        part[ntb + t] = v_part[:, LANES * t:LANES * (t + 1)]
     pl.semaphore_wait(barrier, len(greeted))
     relays = [2, ny - 2] if far else []
     for d in relays:
@@ -176,8 +176,7 @@
             some = qall.at[0, pl.ds(0, count), 0]
             pltpu.make_async_copy(some, some, sem).wait()
 
-    def onward(c, near_sems, rest_sems):
-        await_blocks(len(z_near), near_sems[1])
+    def onward(c, rest_sems):
         if z_rest:
             hand(nz - 2, c, 2, rest_sems)
             hand(nz - 2, c, 1, rest_sems)
@@ -206,7 +205,6 @@
     across.wait_recv()
     for d in z_near:
         hand(0, partner, d, p_sems)
-    onward(x, q_sems, q2_sems)
 
     row_id = lax.broadcasted_iota(jnp.int32, (LANES, LANES), 0)
     col_id = lax.broadcasted_iota(jnp.int32, (LANES, LANES), 1)
@@ -225,28 +223,31 @@
     for t in range(ntb):
         gram_part[t] = gram[rows * t:rows * (t + 1)]
 
-    for r in by_distance(range(1, ntb), lambda r: f_far(2 * r)):
+    for r in by_distance(range(1, ntb), f_far):
         to = lax.rem(block + r, ntb)
-        send(gram_part.at[to], ga_buf.at[r - 1], ga_sems, {"fsdp": 2 * to + side})
+        send(gram_part.at[to], ga_buf.at[r - 1], ga_sems, {"fsdp": side * ntb + to})
+
+    await_blocks(len(z_near), q_sems[1])
+    await_blocks(len(z_near), p_sems[1])
+    pltpu.make_async_copy(ga_buf, ga_buf, ga_sems[1]).wait()
+    gsum = gram_part[block]
+    for r in range(ntb - 1):
+        gsum = gsum + ga_buf[r]
+    gb_own[0] = gsum
+    twin = send(gb_own.at[0], gs_buf, gs_sems, sibling)
     for d in far:
         send(chunks.at[f], chunks.at[f], far_sems, {"fsdp": place_of(col, d)})
     for d in near:
         for c in (other, col):
             send(chunks.at[f], chunks.at[f], ag_sems, {"fsdp": place_of(c, d)})
     send(chunks.at[f], chunks.at[f], ag_sems, pair_f)
-
-    onward(partner, p_sems, p2_sems)
-    pltpu.make_async_copy(ga_buf, ga_buf, ga_sems[1]).wait()
-    gsum = gram_part[block]
-    for r in range(ntb - 1):
-        gsum = gsum + ga_buf[r]
-    gb_own[0] = gsum
-    twin = send(gb_own.at[0], gs_buf, gs_sems, sibling)
     twin.wait_recv()
     gsum = gsum + gs_buf[...]
     gb_own[1] = gsum
     for r in d_steps:
         send(gb_own.at[1], gb_buf.at[r - 1], gb_sems, over_d(r))
+    onward(x, q2_sems)
+    onward(partner, p2_sems)
     far_chunks = chunks.at[pl.ds(0, len(far))]
     if far:
         pltpu.make_async_copy(far_chunks, far_chunks, far_sems[1]).wait()
@@ -257,22 +258,19 @@
     pltpu.make_async_copy(gb_buf, gb_buf, gb_sems[1]).wait()
     for r in range(nch - 1):
         gsum = gsum + gb_buf[r]
-    place = side * ntb + block
+    place = f
     gfull[place] = gsum
 
     for r in f_steps:
         send(gfull.at[place], gfull.at[place], gc_sems, over_f(r))
 
-    await_blocks(len(z_rest), q2_sems[1])
-    await_blocks(len(z_rest), p2_sems[1])
-    twin_q = send(qall.at[core], qall.at[core], sib_sems, sibling)
 
     near_chunks = chunks.at[pl.ds(0, 1 + 2 * len(near))]
     pltpu.make_async_copy(near_chunks, near_chunks, ag_sems[1]).wait()
     if far:
         pltpu.make_async_copy(far_chunks, far_chunks, hand_sems[1]).wait()
-    u_high, u_low = halves(jnp.concatenate([chunks[2 * t] for t in range(ntb)], axis=1))
-    v_high, v_low = halves(jnp.concatenate([chunks[2 * t + 1] for t in range(ntb)], axis=1))
+    u_high, u_low = halves(jnp.concatenate([chunks[t] for t in range(ntb)], axis=1))
+    v_high, v_low = halves(jnp.concatenate([chunks[ntb + t] for t in range(ntb)], axis=1))
     v_both = jnp.concatenate([v_high, v_low], axis=0)
     load_ids.wait()
     ids = ids_ref[...]
@@ -285,6 +283,9 @@
         top = bf_dot(v_both, masked_high, NT)
         stage[pl.ds(R * p, R), :] = top[:R] + top[R:] + bf_dot(v_high, masked_low, NT)
 
+    await_blocks(len(z_rest), q2_sems[1])
+    await_blocks(len(z_rest), p2_sems[1])
+    twin_q = send(qall.at[core], qall.at[core], sib_sems, sibling)
     all_grams = gfull.at[pl.ds(0, nf - 1)]
     pltpu.make_async_copy(all_grams, all_grams, gc_sems[1]).wait()
     inv = inverse_pair(jnp.concatenate([gfull[t] for t in range(nf)], axis=0), eye, left_half, 1.0 / tokens_all)

time: 52.6 us -> 51.5 us (0.979)
  Pallas kernels: 50.9 us -> 49.9 us
    pallas_call x1, Pallas kernels: 50.9 us -> 49.9 us  [on_device(): pl.pallas_call(functools.partial(kernel, nf, nd, nd * tokens), out_shape=...]
where the time goes in v6:
time: 51.5 us; the launch traced here: 51.4 us
  Pallas kernels  49.9 us (97%)
  local copies, waits for them, and re-layouts  1.47 us (3%)
    pallas_call x1, Pallas kernels, on_device(): pl.pallas_call(functools.partial(kernel, nf, nd, nd * tokens), out_shape=...  49.9 us
    unnamed x1, local copies, waits for them, and re-layouts  1.47 us

profile of v6, /device:TPU:1, one launch (start us, length us, event | category | flops | bytes accessed | tf_op | source)
XLA Modules:
  0.0 51.4 jit_solution(2199091121965340141)
XLA Ops:
  0.0 49.9 %influence.1 = f32[16,8,32]{2,1,0:T(8,128)} custom-call(bf16[1024,512]{1,0:T(8,128)(2,1)} %attn_hbm.1, bf16[1024,1024]{1,0:T(8,128)(2,1)} %cot_hbm.1, bf16[512,1024]{1,0:T(8,128)(2,1)} %kw_hbm.1, bf16[64,512]{1,0:T(8,128)(2,1)} %pin_hbm.1, bf16[64,512]{1,0:T(8,128)(2,1)} %pout_hbm.1, bf16[1,8,4096]{2,1,0:T(8,128)(2,1)} %query_hbm.1, s32[1,32]{1,0:T(1,128)} %bitcast.3, ...), custom_call_target="tpu_custom_call" | custom-call | tf_op jit(solution)/shard_map/influence/pallas_call | solution.py:350
  49.9 1.5 %copy.10 = f32[16,32,8]{1,2,0:T(8,128)} copy(f32[16,32,8]{1,2,0:T(8,128)} %bitcast.2) | data formatting | bytes 32768

commit v7 on v6

--- a/solution.py
+++ b/solution.py
@@ -237,15 +237,15 @@
     twin = send(gb_own.at[0], gs_buf, gs_sems, sibling)
     for d in far:
         send(chunks.at[f], chunks.at[f], far_sems, {"fsdp": place_of(col, d)})
-    for d in near:
-        for c in (other, col):
-            send(chunks.at[f], chunks.at[f], ag_sems, {"fsdp": place_of(c, d)})
-    send(chunks.at[f], chunks.at[f], ag_sems, pair_f)
     twin.wait_recv()
     gsum = gsum + gs_buf[...]
     gb_own[1] = gsum
     for r in d_steps:
         send(gb_own.at[1], gb_buf.at[r - 1], gb_sems, over_d(r))
+    for d in near:
+        for c in (other, col):
+            send(chunks.at[f], chunks.at[f], ag_sems, {"fsdp": place_of(c, d)})
+    send(chunks.at[f], chunks.at[f], ag_sems, pair_f)
     onward(x, q2_sems)
     onward(partner, p2_sems)
     far_chunks = chunks.at[pl.ds(0, len(far))]

time: 51.5 us -> 51.2 us (level)
  no operation moved by 1% of the time
where the time goes in v7:
time: 51.2 us; the launch traced here: 51.1 us
  Pallas kernels  49.6 us (97%)
  local copies, waits for them, and re-layouts  1.47 us (3%)
    pallas_call x1, Pallas kernels, on_device(): pl.pallas_call(functools.partial(kernel, nf, nd, nd * tokens), out_shape=...  49.6 us
    unnamed x1, local copies, waits for them, and re-layouts  1.47 us

profile of v7, /device:TPU:1, one launch (start us, length us, event | category | flops | bytes accessed | tf_op | source)
XLA Modules:
  0.0 51.1 jit_solution(1048586516051746631)
XLA Ops:
  0.0 49.6 %influence.1 = f32[16,8,32]{2,1,0:T(8,128)} custom-call(bf16[1024,512]{1,0:T(8,128)(2,1)} %attn_hbm.1, bf16[1024,1024]{1,0:T(8,128)(2,1)} %cot_hbm.1, bf16[512,1024]{1,0:T(8,128)(2,1)} %kw_hbm.1, bf16[64,512]{1,0:T(8,128)(2,1)} %pin_hbm.1, bf16[64,512]{1,0:T(8,128)(2,1)} %pout_hbm.1, bf16[1,8,4096]{2,1,0:T(8,128)(2,1)} %query_hbm.1, s32[1,32]{1,0:T(1,128)} %bitcast.3, ...), custom_call_target="tpu_custom_call" | custom-call | tf_op jit(solution)/shard_map/influence/pallas_call | solution.py:350
  49.6 1.5 %copy.10 = f32[16,32,8]{1,2,0:T(8,128)} copy(f32[16,32,8]{1,2,0:T(8,128)} %bitcast.2) | data formatting | bytes 32768

commit v8 on v7

--- a/solution.py
+++ b/solution.py
@@ -318,8 +318,7 @@
     tail = (rest - mid.astype(F32)).astype(BF16)
     picked = bf_dot(jnp.concatenate([big, mid, tail], axis=0), select[...])
     picked = (picked[:EX] + picked[EX:2 * EX] + picked[2 * EX:]) * (1.0 / (R * R))
-    for i in range(per):
-        out_ref[:, i, :] = picked[:, nd * i:nd * (i + 1)]
+    out_ref[...] = picked
 
     across.wait_send()
     twin.wait_send()
@@ -349,7 +348,7 @@
     vmem = pl.BlockSpec(memory_space=pltpu.VMEM)
     scores = pl.pallas_call(
         functools.partial(kernel, nf, nd, nd * tokens),
-        out_shape=jax.ShapeDtypeStruct((EX, per, nd), F32),
+        out_shape=jax.ShapeDtypeStruct((EX, per * nd), F32),
         in_specs=[hbm] * 8,
         out_specs=vmem,
         scratch_shapes=[
@@ -387,7 +386,7 @@
         attn_out, key_cotangent, key_weight, proj_in, proj_out, query_sketches,
         block_owner.reshape(1, nd), example_ids,
     )
-    return scores.transpose(0, 2, 1)
+    return scores.reshape(EX, per, nd).transpose(0, 2, 1)
 
 
 def solution(mesh):

time: 51.2 us -> 51 us (level)
    unnamed x1 -> x0, local copies, waits for them, and re-layouts: 1.47 us -> none
    reshape x0 -> x1, local copies, waits for them, and re-layouts: none -> 1.43 us  [on_device(): return scores.reshape(EX, per, nd).transpose(0, 2, 1)]
where the time goes in v8:
time: 51 us; the launch traced here: 50.8 us
  Pallas kernels  49.4 us (97%)
  local copies, waits for them, and re-layouts  1.43 us (3%)
    pallas_call x1, Pallas kernels, on_device(): pl.pallas_call(functools.partial(kernel, nf, nd, nd * tokens), out_shape=...  49.4 us
    reshape x1, local copies, waits for them, and re-layouts, on_device(): return scores.reshape(EX, per, nd).transpose(0, 2, 1)  1.43 us

profile of v8, /device:TPU:1, one launch (start us, length us, event | category | flops | bytes accessed | tf_op | source)
XLA Modules:
  0.0 50.8 jit_solution(8948122670215854044)
XLA Ops:
  0.0 49.4 %influence.1 = f32[16,256]{1,0:T(8,128)} custom-call(bf16[1024,512]{1,0:T(8,128)(2,1)} %attn_hbm.1, bf16[1024,1024]{1,0:T(8,128)(2,1)} %cot_hbm.1, bf16[512,1024]{1,0:T(8,128)(2,1)} %kw_hbm.1, bf16[64,512]{1,0:T(8,128)(2,1)} %pin_hbm.1, bf16[64,512]{1,0:T(8,128)(2,1)} %pout_hbm.1, bf16[1,8,4096]{2,1,0:T(8,128)(2,1)} %query_hbm.1, s32[1,32]{1,0:T(1,128)} %bitcast.2, ...), custom_call_target="tpu_custom_call" | custom-call | tf_op jit(solution)/shard_map/influence/pallas_call | solution.py:349
  49.4 1.4 %reshape.7 = f32[16,8,32]{2,1,0:T(8,128)} reshape(f32[16,256]{1,0:T(8,128)} %influence.1) | data formatting | bytes 32768 | tf_op jit(solution)/shard_map/reshape | solution.py:389
